TPU v7x, 128 devices: a whole 4x4x4 slice. The times are simulated.
128 devices in a mesh: dp: 4 (over x), vocab: 32 (over z, y, core).
Axes of the slice: x: 4, y: 4, z: 4, core: 2. Of those that a mesh axis runs over, the one named last changes fastest.
Arguments:
- hidden: bfloat16 [2048, 3584], P('dp'), may hold values from -120 to 120
- head_weight: bfloat16 [3584, 76032], P(None, 'vocab'), may hold values from -0.09375 to 0.09375
- teacher_ids: int32 [2048, 64], P(('dp', 'vocab')), may hold values from 0 to 76031, as said below
- teacher_logits: float32 [2048, 64], P(('dp', 'vocab')), may hold values from -400 to 400
Outputs:
- token_loss: float32 [2048], P('dp')
- grad_hidden: float32 [2048, 3584], P(('dp', 'vocab'))
Inputs may be any that keep to these rules, and one draw needn't show every extreme that they name: `teacher_ids`: each row holds 64 distinct ids in ascending order.
All inputs are finite; a program needn't handle non-finite values.
Results may differ from a plain program's by a relative error of at most 0.0029.
Values sent between devices are 32-bit elements; how exact they have to be, the bound alone decides.
A program may use at most 128 MiB of HBM per device.

v0:
```python
import jax
import jax.numpy as jnp
from jax import lax
from jax.sharding import PartitionSpec as P


def teacher_side(teacher_logits):
    shifted = teacher_logits - jnp.max(teacher_logits, axis=1, keepdims=True)
    log_probs = shifted - jnp.log(jnp.sum(jnp.exp(shifted), axis=1, keepdims=True))
    probs = jnp.exp(log_probs)
    return (probs, jnp.sum(probs * log_probs, axis=1))


def build_target(safe_index, weights, columns):
    rows = safe_index.shape[0]
    block = min(32, rows)
    blocks = rows // block
    column_ids = lax.iota(jnp.int32, columns)

    def one_block(pieces):
        index_block, weight_block = pieces
        matches = column_ids[None, None, :] == index_block[:, :, None]
        spread = jnp.where(matches, weight_block[:, :, None], jnp.float32(0.0))
        return jnp.sum(spread, axis=1)

    shaped = (safe_index.reshape(blocks, block, -1), weights.reshape(blocks, block, -1))
    return lax.map(one_block, shaped).reshape(rows, columns)


def local(hidden, head_weight, teacher_ids, teacher_logits):
    columns = head_weight.shape[1]
    offset = lax.axis_index("vocab") * columns
    gathered_ids, gathered_logits = (
        lax.all_gather(teacher_ids, "vocab", axis=0, tiled=True),
        lax.all_gather(teacher_logits, "vocab", axis=0, tiled=True),
    )
    probs, negent = teacher_side(gathered_logits)
    logits = jnp.dot(hidden, head_weight, preferred_element_type=jnp.float32)
    local_ids = gathered_ids - offset
    inside = (local_ids >= 0) & (local_ids < columns)
    safe_index = jnp.where(inside, local_ids, 0).astype(jnp.int32)
    weights = jnp.where(inside, probs, jnp.zeros_like(probs))
    target = build_target(safe_index, weights, columns)
    cross_part = jnp.sum(target * logits, axis=1)
    row_top = lax.pmax(jnp.max(logits, axis=1), "vocab")
    exp_sum = jnp.sum(jnp.exp(logits - row_top[:, None]), axis=1)
    total, cross = lax.psum((exp_sum, cross_part), "vocab")
    log_total = row_top + jnp.log(total)
    token_loss = negent - cross + log_total
    grad_logits = (jnp.exp(logits - log_total[:, None]) - target).astype(jnp.bfloat16)
    share = logits.shape[0] // lax.axis_size("vocab")
    term = lax.dot_general(
        grad_logits, head_weight, (((1,), (1,)), ((), ())), preferred_element_type=jnp.float32
    )
    summed = lax.psum(term, "vocab")
    own_rows = lax.dynamic_slice_in_dim(summed, lax.axis_index("vocab") * share, share, 0)
    return (token_loss, own_rows)


def solution(mesh):
    placed = (P("dp", None), P(None, "vocab"), P(("dp", "vocab"), None), P(("dp", "vocab"), None))
    return jax.shard_map(
        local,
        mesh=mesh,
        in_specs=placed,
        out_specs=(P("dp"), P(("dp", "vocab"), None)),
        check_vma=False,
    )
```

profile of v0, /device:TPU:0, one launch (start us, length us, event | category | flops | bytes accessed | tf_op | source)
XLA Modules:
  0.0 431.1 jit_solution(16632105482492170738)
XLA Ops:
  7.2 0.0 all-reduce.3.cloned.1.call-start
  7.2 26.4 %all_gather.6 = f32[512,64]{1,0:T(8,128)S(1)} all-gather(f32[16,64]{1,0:T(8,128)} %param.9), channel_id=1, replica_groups=mesh['dp'=4,'vocab'=32] {'vocab'}, dimensions={0}, use_global_device_ids=true | all-gather | bytes 135168 | tf_op jit(solution)/shard_map/all_gather | solution.py:35
  33.6 24.2 %all_gather.7 = s32[512,64]{1,0:T(8,128)S(1)} all-gather(s32[16,64]{1,0:T(8,128)} %param.8), channel_id=1, replica_groups=mesh['dp'=4,'vocab'=32] {'vocab'}, dimensions={0}, use_global_device_ids=true | all-gather | bytes 135168 | tf_op jit(solution)/shard_map/all_gather | solution.py:34
  57.8 0.1 reduce_max.18
  57.9 0.2 exponential_reduce_fusion.1
  58.3 0.3 exponential_select_fusion
  58.6 76.4 %while.11 = (s32[]{:T(128)}, f32[16,32,2376]{2,1,0:T(8,128)}, s32[16,32,64]{2,1,0:T(8,128)S(1)}, f32[16,32,64]{2,1,0:T(8,128)S(1)}, s32[]{:T(128)}) while((s32[]{:T(128)}, f32[16,32,2376]{2,1,0:T(8,128)}, s32[16,32,64]{2,1,0:T(8,128)S(1)}, f32[16,32,64]{2,1,0:T(8,128)S(1)}, s32[]{:T(128)}) %tuple.35), condition=%wide.region_5.6_spmd.clone, body=%wide.region_3.5_spmd.clone.sunk | while | flops 14522114 | bytes 968785 | solution.py:27
  58.6 4.0 select_reduce_fusion.2
  62.6 0.7 bitcast_dynamic-update-slice_fusion.2
  63.4 4.0 select_reduce_fusion.2
  67.4 0.7 bitcast_dynamic-update-slice_fusion.2
  68.1 4.0 select_reduce_fusion.2
  72.2 0.7 bitcast_dynamic-update-slice_fusion.2
  72.9 4.0 select_reduce_fusion.2
  76.9 0.7 bitcast_dynamic-update-slice_fusion.2
  77.7 4.0 select_reduce_fusion.2
  81.7 0.8 bitcast_dynamic-update-slice_fusion.2
  82.5 4.0 select_reduce_fusion.2
  86.5 0.7 bitcast_dynamic-update-slice_fusion.2
  87.2 4.0 select_reduce_fusion.2
  91.3 0.7 bitcast_dynamic-update-slice_fusion.2
  92.0 4.0 select_reduce_fusion.2
  96.0 0.7 bitcast_dynamic-update-slice_fusion.2
  96.8 4.0 select_reduce_fusion.2
  100.8 0.8 bitcast_dynamic-update-slice_fusion.2
  101.5 4.0 select_reduce_fusion.2
  105.6 0.8 bitcast_dynamic-update-slice_fusion.2
  106.3 4.0 select_reduce_fusion.2
  110.4 0.8 bitcast_dynamic-update-slice_fusion.2
  111.1 4.0 select_reduce_fusion.2
  115.1 0.7 bitcast_dynamic-update-slice_fusion.2
  115.9 4.0 select_reduce_fusion.2
  119.9 0.7 bitcast_dynamic-update-slice_fusion.2
  120.7 4.0 select_reduce_fusion.2
  124.7 0.7 bitcast_dynamic-update-slice_fusion.2
  125.4 4.0 select_reduce_fusion.2
  129.5 0.7 bitcast_dynamic-update-slice_fusion.2
  130.2 4.0 select_reduce_fusion.2
  134.2 0.8 bitcast_dynamic-update-slice_fusion.2
  135.0 5.8 %copy.9 = f32[512,2376]{0,1:T(8,128)} copy(f32[512,2376]{1,0:T(8,128)} %bitcast.18) | data formatting | bytes 9732096 | tf_op jit(solution)/shard_map/reshape | solution.py:27
  140.8 14.4 %fusion.5 = (f32[512]{0:T(512)S(1)}, f32[512,2376]{0,1:T(8,128)}) fusion(bf16[512,3584]{1,0:T(8,128)(2,1)} %param.6, bf16[3584,2376]{0,1:T(8,128)(2,1)} %param.7), kind=kOutput, calls=%fused_computation.20 | convolution fusion | flops 8721174528 | bytes 25569280 | tf_op jit(solution)/shard_map/dot_general | solution.py:38
  155.2 65.3 %pmax.7 = f32[512]{0:T(512)S(1)} all-reduce(f32[512]{0:T(512)S(1)} %get-tuple-element.56), channel_id=1, replica_groups=mesh['dp'=4,'vocab'=32] {'vocab'}, use_global_device_ids=true, to_apply=%region_9.10 | all-reduce | flops 512 | bytes 4096 | tf_op jit(solution)/shard_map/pmax | solution.py:45
  220.4 4.9 %multiply_reduce_fusion = (f32[512]{0:T(512)S(1)}, f32[512]{0:T(512)S(1)}) fusion(f32[512,2376]{0,1:T(8,128)} %copy.9, f32[512,2376]{0,1:T(8,128)} %get-tuple-element.57, f32[512]{0:T(512)S(1)} %pmax.7), kind=kLoop, calls=%fused_computation.8 | loop fusion | flops 4865024 | bytes 9738240 | tf_op jit(solution)/shard_map/reduce_sum | solution.py:44
  225.4 62.8 %all-reduce = (f32[512]{0:T(512)S(1)}, f32[512]{0:T(512)S(1)}) all-reduce(f32[512]{0:T(512)S(1)} %get-tuple-element.41, f32[512]{0:T(512)S(1)} %get-tuple-element.40), channel_id=1, replica_groups=mesh['dp'=4,'vocab'=32] {'vocab'}, use_global_device_ids=true, to_apply=%region_11.12 | all-reduce | flops 1024 | bytes 8192 | tf_op jit(solution)/shard_map/psum | solution.py:47
  288.2 0.6 subtract_add_fusion
  288.8 18.9 %fusion.2 = f32[512,3584]{1,0:T(8,128)} fusion(bf16[3584,2376]{0,1:T(8,128)(2,1)} %param.7, f32[512,2376]{0,1:T(8,128)} %copy.9, f32[512,2376]{0,1:T(8,128)} %get-tuple-element.57, f32[512]{0:T(512)S(1)} %get-tuple-element.53), kind=kOutput, calls=%fused_computation.9 | convolution fusion | flops 8723607552 | bytes 34105344 | tf_op jit(solution)/shard_map/dot_general | solution.py:52
  307.7 0.0 all-reduce.3.cloned.1.call-update
  307.8 114.8 %all-reduce.3.cloned.1.call-done = f32[512,3584]{1,0:T(8,128)} async-done(((f32[512,3584]{1,0:T(8,128)}), f32[512,3584]{1,0:T(8,128)}) %all-reduce.3.cloned.1.call-update) | async-done | bytes 7340048 | tf_op jit(solution)/shard_map/psum | solution.py:55
  422.6 1.6 constant_dynamic-slice_fusion
  (35 shorter events, 0.1 us)
Async XLA Ops:
  7.2 415.4 %all-reduce.3.cloned.1.call-start = ((), (), s32[]{:S(2)}) async-start(), calls=%async_computation | async-start | bytes 14680064 | tf_op jit(solution)/shard_map/psum | solution.py:55
Sparse Core Ops, SparseCore 0:
  307.9 114.6 all-reduce.2
where the time goes:
time: 432 us; the launch traced here: 431 us
  blocking collectives  179 us (41%)
  waiting for transfers between devices  115 us (27%)
  other arithmetic  70.5 us (16%)
  matrix products  33.3 us (8%)
  local copies, waits for them, and re-layouts  19.5 us (5%)
  between operations  14.1 us (3%)
    psum x1, waiting for transfers between devices, local(): summed = lax.psum(term, 'vocab')  115 us
    pmax x1, blocking collectives, local(): row_top = lax.pmax(jnp.max(logits, axis=1), 'vocab')  65.3 us
    reduce_sum x16, other arithmetic, one_block(): return jnp.sum(spread, axis=1)  64.2 us
    psum x1, blocking collectives, local(): total, cross = lax.psum((exp_sum, cross_part), 'vocab')  62.8 us
    all_gather x1, blocking collectives, local(): lax.all_gather(teacher_logits, 'vocab', axis=0, tiled=True)  26.4 us
    all_gather x1, blocking collectives, local(): lax.all_gather(teacher_ids, 'vocab', axis=0, tiled=True)  24.2 us
    dot_general x1, matrix products, local(): lax.dot_general(grad_logits, head_weight, (((1,), (1,)), ((), ())), prefe...  18.9 us
    dot_general x1, matrix products, local(): logits = jnp.dot(hidden, head_weight, preferred_element_type=jnp.float32)  14.4 us
  transfers between devices with their start and end apart: 1, of which 1 were waited for; matrix products, arithmetic and copies ran while one was open for 0% of the time, Pallas kernels for 0%

commit v1 on v0

v1 whole, which is shorter than its diff:
```python
import functools

import jax
import jax.numpy as jnp
from jax import lax
from jax.experimental import pallas as pl
from jax.experimental.pallas import tpu as pltpu
from jax.sharding import PartitionSpec as P

MESH = pl.DeviceIdType.MESH
NV = 32
TOK = 512
HALF = 256
OWN = 16
D = 3584
COLS = 2376
MAIN = 2304
TAIL = COLS - MAIN
PADDED = MAIN + 128
TILES = PADDED // 128
DEPTH = 512
NB = D // DEPTH
CW = 512
NC = D // CW
K = 64
NT = (((1,), (1,)), ((), ()))


def slot_of(index):
    core, y, z = index % 2, (index // 2) % 4, index // 8
    return core * 16 + (y * 4 + z) * (1 - core) + (z * 4 + y) * core


def kernel(
    hidden, weight, ids_ref, tlog_ref,
    grad_out, loss_out,
    w, h, logits, target, gm, gt, g, cr, r11, r12, r21, r22,
    comb, stats, ltcol, lsecol, crosscol,
    h_sem, w_sem, comb_send, comb_recv, st_send, st_recv,
    c_send, c_recv, p_send, p_recv,
):
    me = lax.axis_index("vocab")
    core = me % 2
    y = (me // 2) % 4
    z = me // 8
    a = y * (1 - core) + z * core
    b = z * (1 - core) + y * core
    stride_a = 1 + 3 * core
    stride_b = 4 - 3 * core

    def device(a_pos, b_pos):
        return {"vocab": (a_pos * stride_a + b_pos * stride_b) * 2 + core}

    mate = {"vocab": me + 1 - 2 * core}
    a_right, a_left = (a + 1) % 4, (a + 3) % 4
    b_right, b_left = (b + 1) % 4, (b + 3) % 4
    my_slot = core * 16 + a * 4 + b

    for v in range(NV):
        s = slot_of(v)
        pltpu.make_async_copy(hidden.at[pl.ds(v * OWN, OWN)], h.at[pl.ds(s * OWN, OWN)], h_sem).start()

    def w_copy(n):
        rows = pl.ds(n * DEPTH, DEPTH)
        return pltpu.make_async_copy(weight.at[rows], w.at[rows], w_sem.at[n])

    for n in range(NB):
        w_copy(n).start()

    barrier = pltpu.get_barrier_semaphore()
    for d in range(1, NV):
        pl.semaphore_signal(barrier, inc=1, device_id={"vocab": (me + d) % NV}, device_id_type=MESH)
    tl = tlog_ref[...]
    shifted = tl - jnp.max(tl, axis=1, keepdims=True)
    log_probs = shifted - jnp.log(jnp.sum(jnp.exp(shifted), axis=1, keepdims=True))
    probs = jnp.exp(log_probs)
    negent = jnp.sum(probs * log_probs, axis=1, keepdims=True)
    comb[my_slot] = jnp.concatenate([ids_ref[...].astype(jnp.float32), probs], axis=1)
    pl.semaphore_wait(barrier, NV - 1)

    def comb_copy(d):
        return pltpu.make_async_remote_copy(
            comb.at[my_slot], comb.at[my_slot], comb_send, comb_recv,
            device_id={"vocab": (me + d) % NV}, device_id_type=MESH)

    for d in range(1, NV):
        comb_copy(d).start()

    pltpu.make_async_copy(h, h, h_sem).wait()

    for n in range(NB):
        w_copy(n).wait()
        deep = slice(n * DEPTH, (n + 1) * DEPTH)

        @pl.loop(0, MAIN // 256)
        def _(k):
            cols = pl.ds(pl.multiple_of(k * 256, 256), 256)
            part = jnp.dot(h[:, deep], w[deep, cols], preferred_element_type=jnp.float32)
            logits[:, cols] = part if n == 0 else logits[:, cols] + part

        part = jnp.dot(h[:, deep], w[deep, MAIN:], preferred_element_type=jnp.float32)
        logits[:, MAIN:COLS] = part if n == 0 else logits[:, MAIN:COLS] + part

    lane = lax.broadcasted_iota(jnp.int32, (8, 128), 1)

    @pl.loop(0, TOK // 8, unroll=4)
    def _(i):
        rows = pl.ds(pl.multiple_of(i * 8, 8), 8)
        tiles = [logits[rows, t * 128:(t + 1) * 128] for t in range(TILES)]
        tiles[-1] = jnp.where(lane < TAIL, tiles[-1], jnp.float32(-1e30))
        top = functools.reduce(jnp.maximum, tiles)
        m = jnp.max(top, axis=1, keepdims=True)
        acc = functools.reduce(jnp.add, [jnp.exp(t - m) for t in tiles])
        s = jnp.sum(acc, axis=1, keepdims=True)
        lsecol[rows, :] = jnp.broadcast_to(m + jnp.log(s), (8, 128))

    def original_rows(col, i):
        return jnp.concatenate([col[pl.ds(slot_of(8 * i + j) * OWN, OWN), :] for j in range(8)], axis=0)

    for i in range(4):
        stats[0, my_slot, pl.ds(i, 1), :] = jnp.transpose(original_rows(lsecol, i))[0:1, :]

    def stat_copy(k, d):
        return pltpu.make_async_remote_copy(
            stats.at[k, my_slot], stats.at[k, my_slot], st_send.at[k], st_recv.at[k],
            device_id={"vocab": (me + d) % NV}, device_id_type=MESH)

    for d in range(1, NV):
        stat_copy(0, d).start()

    pltpu.make_async_copy(comb.at[0:NV - 1], comb.at[0:NV - 1], comb_recv).wait()
    first = (me * COLS).astype(jnp.float32)
    lane_f = lane.astype(jnp.float32)

    def pick(table, pos):
        return jnp.take_along_axis(table, pos, axis=1)

    @pl.loop(0, TOK // 8)
    def _(i):
        rows = pl.ds(pl.multiple_of(i * 8, 8), 8)
        table = comb[i // 2, pl.ds(pl.multiple_of((i % 2) * 8, 8), 8), :]
        shape = (8, 128)
        mid = jnp.broadcast_to(table[:, 31:32], shape)
        low = jnp.broadcast_to(table[:, 15:16], shape)
        high = jnp.broadcast_to(table[:, 47:48], shape)
        cross = jnp.zeros(shape, jnp.float32)
        for t in range(TILES):
            col = lane_f + (first + jnp.float32(t * 128))
            c = mid < col
            pos = jnp.where(c, 32, 0)
            probe = jnp.where(c, high, low)
            pos = pos + jnp.where(probe < col, 16, 0)
            for s in (8, 4, 2, 1):
                probe = pick(table, pos + (s - 1))
                pos = pos + jnp.where(probe < col, s, 0)
            hit = pick(table, pos) == col
            if t == TILES - 1:
                hit = hit & (lane < TAIL)
            value = jnp.where(hit, pick(table, pos + K), jnp.float32(0.0))
            target[rows, t * 128:(t + 1) * 128] = value
            cross = cross + value * logits[rows, t * 128:(t + 1) * 128]
        crosscol[rows, :] = jnp.broadcast_to(jnp.sum(cross, axis=1, keepdims=True), shape)

    own_rows = pl.ds(pl.multiple_of(my_slot * OWN, OWN), OWN)
    crosscol[own_rows, :] = crosscol[own_rows, :] - negent
    for i in range(4):
        stats[1, my_slot, pl.ds(i, 1), :] = jnp.transpose(original_rows(crosscol, i))[0:1, :]
    for d in range(1, NV):
        stat_copy(1, d).start()

    pltpu.make_async_copy(stats.at[0, 0:NV - 1], stats.at[0, 0:NV - 1], st_recv.at[0]).wait()
    lse = stats[0]
    top = jnp.max(lse, axis=0)
    log_total = top + jnp.log(jnp.sum(jnp.exp(lse - top[None]), axis=0))
    for i in range(4):
        col = jnp.transpose(jnp.broadcast_to(log_total[i:i + 1, :], (128, 128)))
        for j in range(8):
            ltcol[pl.ds(slot_of(8 * i + j) * OWN, OWN), :] = col[j * OWN:(j + 1) * OWN, :]

    lane16 = lax.broadcasted_iota(jnp.int32, (16, 128), 1)

    def make_grad(which):
        @pl.loop(0, HALF // 16)
        def _(i):
            rows = pl.ds(pl.multiple_of(which * HALF + i * 16, 16), 16)
            here = pl.ds(pl.multiple_of(i * 16, 16), 16)
            lt = ltcol[rows, :]
            for t in range(TILES):
                at = slice(t * 128, (t + 1) * 128)
                value = jnp.exp(logits[rows, at] - lt) - target[rows, at]
                if t == TILES - 1:
                    gt[which, here, :] = jnp.where(lane16 < TAIL, value, jnp.float32(0.0)).astype(jnp.bfloat16)
                else:
                    gm[which, here, at] = value.astype(jnp.bfloat16)

    def multiply(c, which):
        @pl.loop(0, CW // 256)
        def _(k):
            rows = pl.ds(pl.multiple_of(c * CW + k * 256, 256), 256)
            part = lax.dot_general(gm[which], w[rows, 0:MAIN], NT, preferred_element_type=jnp.float32)
            part = part + lax.dot_general(gt[which, :, 0:TAIL], w[rows, MAIN:COLS], NT, preferred_element_type=jnp.float32)
            g[c, which, :, :, :, pl.ds(pl.multiple_of(k * 256, 256), 256)] = part.reshape(4, 4, OWN, 256)

    make_grad(1 - core)
    make_grad(core)

    def remote(src, dst, send, recv, where):
        return pltpu.make_async_remote_copy(src, dst, send, recv, device_id=where, device_id_type=MESH)

    def core_copy(c):
        return remote(g.at[c, 1 - core], cr.at[c], c_send.at[c], c_recv.at[c], mate)

    def step11(c):
        far = (a + 2) % 4
        return (
            remote(g.at[c, core, far, 0:2], r11.at[c, 0], p_send.at[c, 0], p_recv.at[c, 0], device(a_right, b)),
            remote(g.at[c, core, far, 2:4], r11.at[c, 1], p_send.at[c, 1], p_recv.at[c, 1], device(a_left, b)),
        )

    def step12(c):
        return (
            remote(g.at[c, core, a_right], r12.at[c, 0], p_send.at[c, 2], p_recv.at[c, 2], device(a_right, b)),
            remote(g.at[c, core, a_left], r12.at[c, 1], p_send.at[c, 3], p_recv.at[c, 3], device(a_left, b)),
        )

    def step21(c):
        far = (b + 2) % 4
        return (
            remote(g.at[c, core, a, far, 0:8], r21.at[c, 0], p_send.at[c, 4], p_recv.at[c, 4], device(a, b_right)),
            remote(g.at[c, core, a, far, 8:16], r21.at[c, 1], p_send.at[c, 5], p_recv.at[c, 5], device(a, b_left)),
        )

    def step22(c):
        return (
            remote(g.at[c, core, a, b_right], r22.at[c, 0], p_send.at[c, 6], p_recv.at[c, 6], device(a, b_right)),
            remote(g.at[c, core, a, b_left], r22.at[c, 1], p_send.at[c, 7], p_recv.at[c, 7], device(a, b_left)),
        )

    def start(copies):
        for copy in copies:
            copy.start()

    def arrived(copies):
        for copy in copies:
            copy.wait_recv()

    def when(i, lag):
        return pl.when((i >= lag) & (i < NC + lag))

    @pl.loop(0, NC + 5)
    def _(i):
        @when(i, 0)
        def _():
            multiply(i, 1 - core)
            core_copy(i).start()
            multiply(i, core)

        @when(i, 1)
        def _():
            c = i - 1
            core_copy(c).wait_recv()
            for k in range(4):
                g[c, core, k] = g[c, core, k] + cr[c, k]
            start(step11(c))

        @when(i, 2)
        def _():
            c = i - 2
            arrived(step11(c))
            g[c, core, a_right, 0:2] = g[c, core, a_right, 0:2] + r11[c, 0]
            g[c, core, a_left, 2:4] = g[c, core, a_left, 2:4] + r11[c, 1]
            start(step12(c))

        @when(i, 3)
        def _():
            c = i - 3
            arrived(step12(c))
            g[c, core, a] = g[c, core, a] + (r12[c, 0] + r12[c, 1])
            start(step21(c))

        @when(i, 4)
        def _():
            c = i - 4
            arrived(step21(c))
            g[c, core, a, b_right, 0:8] = g[c, core, a, b_right, 0:8] + r21[c, 0]
            g[c, core, a, b_left, 8:16] = g[c, core, a, b_left, 8:16] + r21[c, 1]
            start(step22(c))

        @when(i, 5)
        def _():
            c = i - 5
            arrived(step22(c))
            grad_out[:, pl.ds(pl.multiple_of(c * CW, CW), CW)] = g[c, core, a, b] + (r22[c, 0] + r22[c, 1])

    pltpu.make_async_copy(stats.at[1, 0:NV - 1], stats.at[1, 0:NV - 1], st_recv.at[1]).wait()
    loss_out[...] = log_total - jnp.sum(stats[1], axis=0)

    pltpu.make_async_copy(comb.at[0:NV - 1], comb.at[0:NV - 1], comb_send).wait()
    for k in range(2):
        pltpu.make_async_copy(stats.at[k, 0:NV - 1], stats.at[k, 0:NV - 1], st_send.at[k]).wait()

    @pl.loop(0, NC)
    def _(c):
        core_copy(c).wait_send()
        for copy in step11(c) + step12(c) + step21(c) + step22(c):
            copy.wait_send()


def local(hidden, head_weight, teacher_ids, teacher_logits):
    any_space = pl.BlockSpec(memory_space=pl.ANY)
    vmem = pl.BlockSpec(memory_space=pltpu.VMEM)
    f32, bf16 = jnp.float32, jnp.bfloat16
    dma = pltpu.SemaphoreType.DMA
    grad, loss = pl.pallas_call(
        kernel,
        out_shape=(jax.ShapeDtypeStruct((OWN, D), f32), jax.ShapeDtypeStruct((4, 128), f32)),
        in_specs=[any_space, any_space, vmem, vmem],
        out_specs=(vmem, vmem),
        scratch_shapes=[
            pltpu.VMEM((D, COLS), bf16),
            pltpu.VMEM((TOK, D), bf16),
            pltpu.VMEM((TOK, PADDED), f32),
            pltpu.VMEM((TOK, PADDED), f32),
            pltpu.VMEM((2, HALF, MAIN), bf16),
            pltpu.VMEM((2, HALF, 128), bf16),
            pltpu.VMEM((NC, 2, 4, 4, OWN, CW), f32),
            pltpu.VMEM((NC, 4, 4, OWN, CW), f32),
            pltpu.VMEM((NC, 2, 2, OWN, CW), f32),
            pltpu.VMEM((NC, 2, 4, OWN, CW), f32),
            pltpu.VMEM((NC, 2, 8, CW), f32),
            pltpu.VMEM((NC, 2, OWN, CW), f32),
            pltpu.VMEM((NV, OWN, 128), f32),
            pltpu.VMEM((2, NV, 4, 128), f32),
            pltpu.VMEM((TOK, 128), f32),
            pltpu.VMEM((TOK, 128), f32),
            pltpu.VMEM((TOK, 128), f32),
            dma, dma((NB,)), dma, dma, dma((2,)), dma((2,)),
            dma((NC,)), dma((NC,)), dma((NC, 8)), dma((NC, 8)),
        ],
        compiler_params=pltpu.CompilerParams(
            collective_id=0, has_side_effects=True, vmem_limit_bytes=60 * 1024 * 1024),
    )(hidden, head_weight, teacher_ids, teacher_logits)
    return loss.reshape(TOK), grad


def solution(mesh):
    placed = (P("dp", None), P(None, "vocab"), P(("dp", "vocab"), None), P(("dp", "vocab"), None))
    return jax.shard_map(
        local,
        mesh=mesh,
        in_specs=placed,
        out_specs=(P("dp"), P(("dp", "vocab"), None)),
        check_vma=False,
    )
```

time: 432 us -> 147 us (0.34)
  blocking collectives: 179 us -> 0 us
  Pallas kernels: 0 us -> 119 us
  waiting for transfers between devices: 115 us -> 0 us
  other arithmetic: 70.5 us -> 0 us
  matrix products: 33.3 us -> 0 us
  between operations: 14.1 us -> 0.64 us
  local copies, waits for them, and re-layouts: 19.5 us -> 25.7 us
    pallas_call x0 -> x1, Pallas kernels: none -> 119 us  [local(): pl.pallas_call(kernel, out_shape=(jax.ShapeDtypeStruct((OWN, D), f32), ja...]
    psum x1 -> x0, waiting for transfers between devices: 115 us -> none  [local(): summed = lax.psum(term, 'vocab')]
    reduce_sum x18 -> x0, other arithmetic: 69.4 us -> none  [the longest x16 64.2 us: one_block(): return jnp.sum(spread, axis=1)]
    pmax x1 -> x0, blocking collectives: 65.3 us -> none  [local(): row_top = lax.pmax(jnp.max(logits, axis=1), 'vocab')]
    psum x1 -> x0, blocking collectives: 62.8 us -> none  [local(): total, cross = lax.psum((exp_sum, cross_part), 'vocab')]
    all_gather x2 -> x0, blocking collectives: 50.6 us -> none  [the longest x1 26.4 us: local(): lax.all_gather(teacher_logits, 'vocab', axis=0, tiled=True)]
    dot_general x2 -> x0, matrix products: 33.3 us -> none  [the longest x1 18.9 us: local(): lax.dot_general(grad_logits, head_weight, (((1,), (1,)), ((), ())), prefe...]
    unnamed x0 -> x3, local copies, waits for them, and re-layouts: none -> 25.7 us
  transfers between devices with their start and end apart: 1 -> 0, of which waited for: 1 -> 0; matrix products, arithmetic and copies ran while one was open for 0% -> 0% of each run, Pallas kernels for 0% -> 0%
where the time goes in v1:
time: 147 us; the launch traced here: 146 us
  Pallas kernels  119 us (81%)
  local copies, waits for them, and re-layouts  25.7 us (17%)
    pallas_call x1, Pallas kernels, local(): pl.pallas_call(kernel, out_shape=(jax.ShapeDtypeStruct((OWN, D), f32), ja...  119 us
    unnamed x3, local copies, waits for them, and re-layouts  25.7 us

profile of v1, /device:TPU:0, one launch (start us, length us, event | category | flops | bytes accessed | tf_op | source)
XLA Modules:
  0.0 145.8 jit_solution(15403681881123235454)
XLA Ops:
  0.6 22.8 %copy.6.weight = bf16[3584,2376]{1,0:T(8,128)(2,1)} copy(bf16[3584,2376]{0,1:T(8,128)(2,1)} %param.5) | data formatting | bytes 34062336 | tf_op args[1]
  23.4 119.4 %shard_map.59 = (f32[16,3584]{1,0:T(8,128)}, f32[4,128]{1,0:T(4,128)}) custom-call(bf16[512,3584]{1,0:T(8,128)(2,1)} %hidden.1, bf16[3584,2376]{1,0:T(8,128)(2,1)} %copy.6.weight, s32[16,64]{1,0:T(8,128)} %ids_ref.1, f32[16,64]{1,0:T(8,128)} %tlog_ref.1), custom_call_target="tpu_custom_call" | custom-call | tf_op jit(solution)/shard_map/pallas_call | solution.py:314
  142.9 1.3 copy.9
  144.1 1.6 %copy.10 = f32[16,3584]{1,0:T(8,128)} copy(f32[16,3584]{1,0:T(8,128)} %get-tuple-element.9) | data formatting | bytes 458752

commit v2 on v0

v2 whole, which is shorter than its diff:
```python
import functools

import jax
import jax.numpy as jnp
from jax import lax
from jax.experimental import pallas as pl
from jax.experimental.pallas import tpu as pltpu
from jax.sharding import PartitionSpec as P

MESH = pl.DeviceIdType.MESH
NV = 32
TOK = 512
OWN = 16
D = 3584
COLS = 2376
MAIN = 2304
TAIL = COLS - MAIN
PADDED = MAIN + 128
TILES = PADDED // 128
NB = MAIN // 256
UNIT = 256
CHUNKS = (1, 2, 3, 3, 3, 2)
NC = len(CHUNKS)
K = 64
ORDER = (
    "m", "C0", "m", "m", "C1", "X0", "m", "m", "X1", "m", "C2", "m", "Y0", "m", "X2", "m", "C3",
    "Y1", "m", "m", "X3", "Y2", "m", "C4", "Z0", "m", "X4", "Y3", "Z1", "m", "C5", "K1", "Z2", "X5",
    "K2", "Y4", "F0", "K3", "F1", "Z3", "Y5", "K4", "F2", "Z4", "F3", "Z5", "F4", "F5",
)
NT = (((1,), (1,)), ((), ()))


def slot_of(index):
    core, y, z = index % 2, (index // 2) % 4, index // 8
    return core * 16 + (y * 4 + z) * (1 - core) + (z * 4 + y) * core


def kernel(
    hidden, weight, ids_ref, tlog_ref,
    grad_out, loss_out,
    w, h, logits, target, gm, g, cr, r11, r12, r2,
    comb, stat_core, stat_y, stat_z, ltcol, lsecol, crosscol,
    h_sem, w_sem, comb_send, comb_recv, st_send, st_recv, g_send, g_recv,
):
    me = lax.axis_index("vocab")
    core = me % 2
    y = (me // 2) % 4
    z = me // 8
    a = y * (1 - core) + z * core
    b = z * (1 - core) + y * core
    stride_a = 1 + 3 * core
    stride_b = 4 - 3 * core

    def device(a_pos, b_pos):
        return {"vocab": (a_pos * stride_a + b_pos * stride_b) * 2 + core}

    def on_y(d):
        return {"vocab": (z * 4 + (y + d) % 4) * 2 + core}

    def on_z(d):
        return {"vocab": (((z + d) % 4) * 4 + y) * 2 + core}

    def remote(src, dst, send, recv, where):
        return pltpu.make_async_remote_copy(src, dst, send, recv, device_id=where, device_id_type=MESH)

    mate = {"vocab": me + 1 - 2 * core}
    a_right, a_left = (a + 1) % 4, (a + 3) % 4
    my_slot = core * 16 + a * 4 + b

    def start(copies):
        for copy in copies:
            copy.start()

    def arrived(copies):
        for copy in copies:
            copy.wait_recv()

    def left(copies):
        for copy in copies:
            copy.wait_send()

    for v in range(NV):
        s = slot_of(v)
        pltpu.make_async_copy(hidden.at[pl.ds(v * OWN, OWN)], h.at[pl.ds(s * OWN, OWN)], h_sem).start()

    def w_copy(n):
        rows = pl.ds(n * 256, 256)
        return pltpu.make_async_copy(weight.at[rows], w.at[rows], w_sem.at[n])

    def w_tail():
        rows = pl.ds(MAIN, TAIL)
        return pltpu.make_async_copy(weight.at[rows], w.at[rows], w_sem.at[NB])

    for n in range(NB):
        w_copy(n).start()
    w_tail().start()

    barrier = pltpu.get_barrier_semaphore()
    for where in [mate] + [on_y(d) for d in (1, 2, 3)] + [on_z(d) for d in (1, 2, 3)]:
        pl.semaphore_signal(barrier, inc=1, device_id=where, device_id_type=MESH)
    tl = tlog_ref[...]
    shifted = tl - jnp.max(tl, axis=1, keepdims=True)
    log_probs = shifted - jnp.log(jnp.sum(jnp.exp(shifted), axis=1, keepdims=True))
    probs = jnp.exp(log_probs)
    negent = jnp.sum(probs * log_probs, axis=1, keepdims=True)
    ids = ids_ref[...].astype(jnp.float32)
    for i in range(2):
        for t in range(8):
            token = slice(i * 8 + t, i * 8 + t + 1)
            comb[z, y, core, i:i + 1, t * K:(t + 1) * K] = ids[token]
            comb[z, y, core, 2 + i:3 + i, t * K:(t + 1) * K] = probs[token]

    def comb_copies(k):
        if k == 0:
            block = comb.at[z, y, core]
            return [remote(block, block, comb_send.at[0], comb_recv.at[0], mate)]
        block = comb.at[z, y] if k == 1 else comb.at[z]
        return [
            remote(block, block, comb_send.at[3 * k - 3 + d], comb_recv.at[3 * k - 3 + d], (on_y if k == 1 else on_z)(d))
            for d in (1, 2, 3)
        ]

    pltpu.make_async_copy(h, h, h_sem).wait()

    def logits_block(n):
        w_copy(n).wait()
        block = pl.ds(pl.multiple_of(n * 256, 256), 256)
        logits[:, block] = lax.dot_general(h[...], w[block, :], NT, preferred_element_type=jnp.float32)

    pl.loop(0, 2)(logits_block)
    pl.semaphore_wait(barrier, 7)
    start(comb_copies(0))
    pl.loop(2, 4)(logits_block)
    arrived(comb_copies(0))
    start(comb_copies(1))
    pl.loop(4, 7)(logits_block)
    arrived(comb_copies(1))
    start(comb_copies(2))
    pl.loop(7, NB)(logits_block)

    w_tail().wait()
    w[COLS:, :] = jnp.zeros((PADDED - COLS, D), jnp.bfloat16)
    logits[:, MAIN:] = lax.dot_general(h[...], w[MAIN:, :], NT, preferred_element_type=jnp.float32)

    lane = lax.broadcasted_iota(jnp.int32, (8, 128), 1)

    @pl.loop(0, TOK // 8, unroll=8)
    def _(i):
        rows = pl.ds(pl.multiple_of(i * 8, 8), 8)
        tiles = [logits[rows, t * 128:(t + 1) * 128] for t in range(TILES)]
        tiles[-1] = jnp.where(lane < TAIL, tiles[-1], jnp.float32(-1e30))
        top = functools.reduce(jnp.maximum, tiles)
        m = jnp.max(top, axis=1, keepdims=True)
        acc = functools.reduce(jnp.add, [jnp.exp(t - m) for t in tiles])
        s = jnp.sum(acc, axis=1, keepdims=True)
        lsecol[rows, :] = jnp.broadcast_to(m + jnp.log(s), (8, 128))

    def original_rows(col, i):
        return jnp.concatenate([col[pl.ds(slot_of(8 * i + j) * OWN, OWN), :] for j in range(8)], axis=0)

    def in_rows(col):
        return jnp.concatenate([jnp.transpose(original_rows(col, i))[0:1, :] for i in range(4)], axis=0)

    def stat_copies(which, k):
        if k == 0:
            block = stat_core.at[which, core]
            return [remote(block, block, st_send.at[which, 0], st_recv.at[which, 0], mate)]
        block = stat_y.at[which, y] if k == 1 else stat_z.at[which, z]
        return [
            remote(block, block, st_send.at[which, 3 * k - 3 + d], st_recv.at[which, 3 * k - 3 + d], (on_y if k == 1 else on_z)(d))
            for d in (1, 2, 3)
        ]

    def log_add(stats):
        top = jnp.max(stats, axis=0)
        return top + jnp.log(jnp.sum(jnp.exp(stats - top[None]), axis=0))

    stat_core[0, core] = in_rows(lsecol)
    start(stat_copies(0, 0))

    arrived(comb_copies(2))
    first = (me * COLS).astype(jnp.float32)
    bf16 = jnp.bfloat16
    row16 = lax.broadcasted_iota(jnp.int32, (16, 256), 0)
    lane256 = lax.broadcasted_iota(jnp.int32, (16, 256), 1)
    same_token = (row16 % 4) == (lane256 // K)
    tile_of_row = [
        (row16 // 4).astype(jnp.float32).astype(bf16),
        ((row16 // 4) ^ 1).astype(jnp.float32).astype(bf16),
    ]
    column_of_row = row16.astype(jnp.float32).astype(bf16)
    zero, one = jnp.zeros((16, 256), bf16), jnp.ones((16, 256), bf16)
    first_four = lax.broadcasted_iota(jnp.int32, (8, 128), 0) < 4

    def wide(row):
        return jnp.broadcast_to(row, (16, 256))

    def target_rows(i):
        rows = pl.ds(pl.multiple_of(i * 8, 8), 8)
        half, slot = i % 2, i // 2
        slot_core, outer, inner = slot // 16, (slot // 4) % 4, slot % 4
        slot_y = outer * (1 - slot_core) + inner * slot_core
        slot_z = inner * (1 - slot_core) + outer * slot_core
        offset = comb[slot_z, slot_y, slot_core, pl.ds(half, 1), :] - first
        inside = (offset >= 0) & (offset < COLS)
        tile = jnp.floor(offset * jnp.float32(1 / 128))
        column = offset - tile * 128
        tile = jnp.where(inside, tile, jnp.float32(-8))
        rest = comb[slot_z, slot_y, slot_core, pl.ds(2 + half, 1), :]
        parts = []
        for _ in range(3):
            parts.append(rest.astype(bf16).astype(jnp.float32))
            rest = rest - parts[-1]
        placed = []
        for k in range(2):
            at = slice(k * 256, (k + 1) * 256)
            tiles = jnp.where(same_token, wide(tile[:, at]), jnp.float32(-8)).astype(bf16) - tile_of_row[k]
            masks = [tiles == bf16(4 * j) for j in range(5)]
            left_side = [jnp.where(m, part, zero) for part in [wide(p[:, at]).astype(bf16) for p in parts] for m in masks]
            columns = wide(column[:, at]).astype(bf16) - column_of_row
            right_side = [jnp.where(columns == bf16(16 * j), one, zero) for j in range(8)]
            out = lax.dot_general(
                jnp.concatenate(left_side, axis=0), jnp.concatenate(right_side, axis=0), NT, preferred_element_type=jnp.float32)
            placed.append(out[0:80] + out[80:160] + out[160:240])
        cross = jnp.zeros((8, 128), jnp.float32)
        for t in range(TILES):
            at, pair = slice(t * 128, (t + 1) * 128), slice(t // 2 * 8, t // 2 * 8 + 8)
            if t % 2 == 0:
                value = jnp.where(first_four, placed[0][pair], placed[1][pair])
            else:
                value = pltpu.roll(jnp.where(first_four, placed[1][pair], placed[0][pair]), 4, 0)
            target[rows, at] = value
            cross = cross + value * logits[rows, at]
        crosscol[rows, :] = jnp.broadcast_to(jnp.sum(cross, axis=1, keepdims=True), (8, 128))

    pl.loop(0, 16, unroll=8)(target_rows)
    arrived(stat_copies(0, 0))
    stat_y[0, y] = log_add(stat_core[0])
    start(stat_copies(0, 1))
    pl.loop(16, 40, unroll=8)(target_rows)
    arrived(stat_copies(0, 1))
    stat_z[0, z] = log_add(stat_y[0])
    start(stat_copies(0, 2))
    pl.loop(40, 64, unroll=8)(target_rows)
    own_rows = pl.ds(pl.multiple_of(my_slot * OWN, OWN), OWN)
    crosscol[own_rows, :] = crosscol[own_rows, :] - negent
    arrived(stat_copies(0, 2))
    log_total = log_add(stat_z[0])
    for i in range(4):
        col = jnp.transpose(jnp.broadcast_to(log_total[i:i + 1, :], (128, 128)))
        for j in range(8):
            ltcol[pl.ds(slot_of(8 * i + j) * OWN, OWN), :] = col[j * OWN:(j + 1) * OWN, :]

    lane16 = lax.broadcasted_iota(jnp.int32, (16, 128), 1)

    @pl.loop(0, TOK // 16)
    def _(i):
        rows = pl.ds(pl.multiple_of(i * 16, 16), 16)
        lt = ltcol[rows, :]
        for t in range(TILES):
            at = slice(t * 128, (t + 1) * 128)
            value = jnp.exp(logits[rows, at] - lt) - target[rows, at]
            if t == TILES - 1:
                value = jnp.where(lane16 < TAIL, value, jnp.float32(0.0))
            gm[rows, at] = value.astype(jnp.bfloat16)

    def multiply(unit):
        c = max(k for k in range(NC) if sum(CHUNKS[:k]) <= unit)
        at = (unit - sum(CHUNKS[:c])) * UNIT
        part = jnp.dot(gm[...], w[:, unit * UNIT:(unit + 1) * UNIT], preferred_element_type=jnp.float32)
        g[c][:, :, :, :, at:at + UNIT] = part.reshape(2, 4, 4, OWN, UNIT)

    def step_core(c):
        return [remote(g[c].at[1 - core], cr[c], g_send.at[c, 0], g_recv.at[c, 0], mate)]

    def step_far(c):
        far = (a + 2) % 4
        return [
            remote(g[c].at[core, far, 0:2], r11[c].at[0], g_send.at[c, 1], g_recv.at[c, 1], device(a_right, b)),
            remote(g[c].at[core, far, 2:4], r11[c].at[1], g_send.at[c, 2], g_recv.at[c, 2], device(a_left, b)),
        ]

    def step_near(c):
        return [
            remote(g[c].at[core, a_right], r12[c].at[0], g_send.at[c, 3], g_recv.at[c, 3], device(a_right, b)),
            remote(g[c].at[core, a_left], r12[c].at[1], g_send.at[c, 4], g_recv.at[c, 4], device(a_left, b)),
        ]

    def step_last(c):
        return [
            remote(g[c].at[core, a, (b + d) % 4], r2[c].at[d - 1], g_send.at[c, 4 + d], g_recv.at[c, 4 + d], device(a, (b + d) % 4))
            for d in (1, 2, 3)
        ]

    unit = 0
    for event in ORDER:
        if event == "m":
            multiply(unit)
            unit += 1
            continue
        kind, c = event[0], int(event[1])
        if kind == "C":
            start(step_core(c))
        elif kind == "X":
            arrived(step_core(c))
            for k in range(4):
                g[c][core, k] = g[c][core, k] + cr[c][k]
            start(step_far(c))
        elif kind == "Y":
            arrived(step_far(c))
            g[c][core, a_right, 0:2] = g[c][core, a_right, 0:2] + r11[c][0]
            g[c][core, a_left, 2:4] = g[c][core, a_left, 2:4] + r11[c][1]
            start(step_near(c))
        elif kind == "Z":
            arrived(step_near(c))
            g[c][core, a] = g[c][core, a] + (r12[c][0] + r12[c][1])
            start(step_last(c))
        elif kind == "F":
            arrived(step_last(c))
            at = sum(CHUNKS[:c]) * UNIT
            grad_out[:, at:at + CHUNKS[c] * UNIT] = g[c][core, a, b] + ((r2[c][0] + r2[c][1]) + r2[c][2])
        elif c == 1:
            stat_core[1, core] = in_rows(crosscol)
            start(stat_copies(1, 0))
        elif c == 2:
            arrived(stat_copies(1, 0))
            stat_y[1, y] = jnp.sum(stat_core[1], axis=0)
            start(stat_copies(1, 1))
        elif c == 3:
            arrived(stat_copies(1, 1))
            stat_z[1, z] = jnp.sum(stat_y[1], axis=0)
            start(stat_copies(1, 2))
        else:
            arrived(stat_copies(1, 2))
            loss_out[...] = log_total - jnp.sum(stat_z[1], axis=0)

    for k in range(3):
        left(comb_copies(k) + stat_copies(0, k) + stat_copies(1, k))
    for c in range(NC):
        left(step_core(c) + step_far(c) + step_near(c) + step_last(c))


def local(hidden, head_weight, teacher_ids, teacher_logits):
    any_space = pl.BlockSpec(memory_space=pl.ANY)
    vmem = pl.BlockSpec(memory_space=pltpu.VMEM)
    f32, bf16 = jnp.float32, jnp.bfloat16
    dma = pltpu.SemaphoreType.DMA
    widths = [k * UNIT for k in CHUNKS]
    grad, loss = pl.pallas_call(
        kernel,
        out_shape=(jax.ShapeDtypeStruct((OWN, D), f32), jax.ShapeDtypeStruct((4, 128), f32)),
        in_specs=[any_space, any_space, vmem, vmem],
        out_specs=(vmem, vmem),
        scratch_shapes=[
            pltpu.VMEM((PADDED, D), bf16),
            pltpu.VMEM((TOK, D), bf16),
            pltpu.VMEM((TOK, PADDED), f32),
            pltpu.VMEM((TOK, PADDED), f32),
            pltpu.VMEM((TOK, PADDED), bf16),
            [pltpu.VMEM((2, 4, 4, OWN, k), f32) for k in widths],
            [pltpu.VMEM((4, 4, OWN, k), f32) for k in widths],
            [pltpu.VMEM((2, 2, OWN, k), f32) for k in widths],
            [pltpu.VMEM((2, 4, OWN, k), f32) for k in widths],
            [pltpu.VMEM((3, OWN, k), f32) for k in widths],
            pltpu.VMEM((4, 4, 2, 4, 8 * K), f32),
            pltpu.VMEM((2, 2, 4, 128), f32),
            pltpu.VMEM((2, 4, 4, 128), f32),
            pltpu.VMEM((2, 4, 4, 128), f32),
            pltpu.VMEM((TOK, 128), f32),
            pltpu.VMEM((TOK, 128), f32),
            pltpu.VMEM((TOK, 128), f32),
            dma, dma((NB + 1,)), dma((7,)), dma((7,)), dma((2, 7)), dma((2, 7)), dma((NC, 8)), dma((NC, 8)),
        ],
        compiler_params=pltpu.CompilerParams(
            collective_id=0, has_side_effects=True, vmem_limit_bytes=60 * 1024 * 1024),
    )(hidden, head_weight.T, teacher_ids, teacher_logits)
    return loss.reshape(TOK), grad


def solution(mesh):
    placed = (P("dp", None), P(None, "vocab"), P(("dp", "vocab"), None), P(("dp", "vocab"), None))
    return jax.shard_map(
        local,
        mesh=mesh,
        in_specs=placed,
        out_specs=(P("dp"), P(("dp", "vocab"), None)),
        check_vma=False,
    )
```

time: 432 us -> 75.3 us (0.17)
  blocking collectives: 179 us -> 0 us
  waiting for transfers between devices: 115 us -> 0 us
  Pallas kernels: 0 us -> 71.4 us
  other arithmetic: 70.5 us -> 0 us
  matrix products: 33.3 us -> 0 us
  local copies, waits for them, and re-layouts: 19.5 us -> 2.89 us
  between operations: 14.1 us -> 0.64 us
    psum x1 -> x0, waiting for transfers between devices: 115 us -> none  [local(): summed = lax.psum(term, 'vocab')]
    pallas_call x0 -> x1, Pallas kernels: none -> 71.4 us  [local(): pl.pallas_call(kernel, out_shape=(jax.ShapeDtypeStruct((OWN, D), f32), ja...]
    reduce_sum x18 -> x0, other arithmetic: 69.4 us -> none  [the longest x16 64.2 us: one_block(): return jnp.sum(spread, axis=1)]
    pmax x1 -> x0, blocking collectives: 65.3 us -> none  [local(): row_top = lax.pmax(jnp.max(logits, axis=1), 'vocab')]
    psum x1 -> x0, blocking collectives: 62.8 us -> none  [local(): total, cross = lax.psum((exp_sum, cross_part), 'vocab')]
    all_gather x2 -> x0, blocking collectives: 50.6 us -> none  [the longest x1 26.4 us: local(): lax.all_gather(teacher_logits, 'vocab', axis=0, tiled=True)]
    dot_general x2 -> x0, matrix products: 33.3 us -> none  [the longest x1 18.9 us: local(): lax.dot_general(grad_logits, head_weight, (((1,), (1,)), ((), ())), prefe...]
    dynamic_update_slice x16 -> x0, local copies, waits for them, and re-layouts: 11.9 us -> none  [build_target(): return lax.map(one_block, shaped).reshape(rows, columns)]
  transfers between devices with their start and end apart: 1 -> 0, of which waited for: 1 -> 0; matrix products, arithmetic and copies ran while one was open for 0% -> 0% of each run, Pallas kernels for 0% -> 0%
where the time goes in v2:
time: 75.3 us; the launch traced here: 74.9 us
  Pallas kernels  71.4 us (95%)
  local copies, waits for them, and re-layouts  2.89 us (4%)
    pallas_call x1, Pallas kernels, local(): pl.pallas_call(kernel, out_shape=(jax.ShapeDtypeStruct((OWN, D), f32), ja...  71.4 us
    unnamed x2, local copies, waits for them, and re-layouts  2.89 us

profile of v2, /device:TPU:0, one launch (start us, length us, event | category | flops | bytes accessed | tf_op | source)
XLA Modules:
  0.0 74.9 jit_solution(8110920506698608314)
XLA Ops:
  0.6 71.4 %shard_map.59 = (f32[16,3584]{1,0:T(8,128)}, f32[4,128]{1,0:T(4,128)}) custom-call(bf16[512,3584]{1,0:T(8,128)(2,1)} %hidden.1, bf16[2376,3584]{1,0:T(8,128)(2,1)} %bitcast.2, s32[16,64]{1,0:T(8,128)} %ids_ref.1, f32[16,64]{1,0:T(8,128)} %tlog_ref.1), custom_call_target="tpu_custom_call" | custom-call | tf_op jit(solution)/shard_map/pallas_call | solution.py:349
  72.0 1.2 %copy.8 = f32[512]{0:T(512)} copy(f32[512]{0:T(512)} %bitcast.3) | data formatting | bytes 4096
  73.2 1.6 %copy.9 = f32[16,3584]{1,0:T(8,128)} copy(f32[16,3584]{1,0:T(8,128)} %get-tuple-element.9) | data formatting | bytes 458752

commit v3 on v2

v3 whole, which is shorter than its diff:
```python
import functools

import jax
import jax.numpy as jnp
from jax import lax
from jax.experimental import pallas as pl
from jax.experimental.pallas import tpu as pltpu
from jax.sharding import PartitionSpec as P

MESH = pl.DeviceIdType.MESH
NV = 32
TOK = 512
OWN = 16
D = 3584
COLS = 2376
MAIN = 2304
TAIL = COLS - MAIN
PADDED = MAIN + 128
TILES = PADDED // 128
NB = MAIN // 256
UNIT = 256
CHUNKS = (1, 2, 3, 3, 3, 2)
NC = len(CHUNKS)
STRAIGHT = (4, 5)
K = 64
ORDER = (
    "m", "m", "m", "C1", "C0", "m", "m", "X1", "m", "C2", "X0", "m", "m", "X2", "m", "C3", "Y1",
    "m", "Y0", "m", "X3", "m", "C4", "Y2", "m", "m", "X4", "C5", "Y3", "K1", "Z2", "X5", "Z0", "Y4",
    "Z3", "Y5", "Z1", "W0", "W2", "Z4", "W3", "Z5", "W1", "K2", "F4", "F3", "F2", "F0", "F5", "K3",
    "F1",
)
NT = (((1,), (1,)), ((), ()))


def slot_of(index):
    core, y, z = index % 2, (index // 2) % 4, index // 8
    return core * 16 + (y * 4 + z) * (1 - core) + (z * 4 + y) * core


def kernel(
    hidden, weight, ids_ref, tlog_ref,
    grad_out, loss_out,
    w, h, logits, target, gm, g, cr, r11, r12, r2,
    comb, stat_core, stat_chip, ltcol, top, total, cross,
    h_sem, w_sem, comb_send, comb_recv, st_send, st_recv, g_send, g_recv,
):
    me = lax.axis_index("vocab")
    core = me % 2
    y = (me // 2) % 4
    z = me // 8
    a = y * (1 - core) + z * core
    b = z * (1 - core) + y * core
    stride_a = 1 + 3 * core
    stride_b = 4 - 3 * core

    def device(a_pos, b_pos):
        return {"vocab": (a_pos * stride_a + b_pos * stride_b) * 2 + core}

    def chip(dy, dz):
        return {"vocab": (((z + dz) % 4) * 4 + (y + dy) % 4) * 2 + core}

    others = [(dy, dz) for dz in range(4) for dy in range(4) if dy or dz]

    def remote(src, dst, send, recv, where):
        return pltpu.make_async_remote_copy(src, dst, send, recv, device_id=where, device_id_type=MESH)

    mate = {"vocab": me + 1 - 2 * core}
    a_right, a_left = (a + 1) % 4, (a + 3) % 4
    b_right, b_left = (b + 1) % 4, (b + 3) % 4
    my_slot = core * 16 + a * 4 + b

    def start(copies):
        for copy in copies:
            copy.start()

    def arrived(copies):
        for copy in copies:
            copy.wait_recv()

    def left(copies):
        for copy in copies:
            copy.wait_send()

    for v in range(NV):
        s = slot_of(v)
        pltpu.make_async_copy(hidden.at[pl.ds(v * OWN, OWN)], h.at[pl.ds(s * OWN, OWN)], h_sem).start()

    def w_copy(n):
        rows = pl.ds(n * 256, 256)
        return pltpu.make_async_copy(weight.at[rows], w.at[rows], w_sem.at[n])

    def w_tail():
        rows = pl.ds(MAIN, TAIL)
        return pltpu.make_async_copy(weight.at[rows], w.at[rows], w_sem.at[NB])

    for n in range(NB):
        w_copy(n).start()
    w_tail().start()

    barrier = pltpu.get_barrier_semaphore()
    for where in [mate] + [chip(dy, dz) for dy, dz in others]:
        pl.semaphore_signal(barrier, inc=1, device_id=where, device_id_type=MESH)
    tl = tlog_ref[...]
    shifted = tl - jnp.max(tl, axis=1, keepdims=True)
    log_probs = shifted - jnp.log(jnp.sum(jnp.exp(shifted), axis=1, keepdims=True))
    probs = jnp.exp(log_probs)
    negent = jnp.sum(probs * log_probs, axis=1, keepdims=True)
    ids = ids_ref[...].astype(jnp.float32)
    for i in range(2):
        for t in range(8):
            token = slice(i * 8 + t, i * 8 + t + 1)
            comb[core, z, y, i:i + 1, t * K:(t + 1) * K] = ids[token]
            comb[core, z, y, 2 + i:3 + i, t * K:(t + 1) * K] = probs[token]

    def comb_copies(k):
        if k == 1:
            return [remote(comb.at[core], comb.at[core], comb_send.at[15], comb_recv.at[15], mate)]
        block = comb.at[core, z, y]
        return [
            remote(block, block, comb_send.at[i], comb_recv.at[i], chip(dy, dz)) for i, (dy, dz) in enumerate(others)
        ]

    def stat_copies(which, k):
        if k == 0:
            block = stat_core.at[which, core]
            return [remote(block, block, st_send.at[which, 15], st_recv.at[which, 15], mate)]
        block = stat_chip.at[which, z * 4 + y]
        return [
            remote(block, block, st_send.at[which, i], st_recv.at[which, i], chip(dy, dz))
            for i, (dy, dz) in enumerate(others)
        ]

    def log_add(stats):
        peak = jnp.max(stats, axis=0)
        return peak + jnp.log(jnp.sum(jnp.exp(stats - peak[None]), axis=0))

    first = (me * COLS).astype(jnp.float32)
    bf16 = jnp.bfloat16
    row16 = lax.broadcasted_iota(jnp.int32, (16, 256), 0)
    lane256 = lax.broadcasted_iota(jnp.int32, (16, 256), 1)
    same_token = (row16 % 4) == (lane256 // K)
    tile_of_row = [
        (row16 // 4).astype(jnp.float32).astype(bf16),
        ((row16 // 4) ^ 1).astype(jnp.float32).astype(bf16),
    ]
    column_of_row = row16.astype(jnp.float32).astype(bf16)
    zero, one = jnp.zeros((16, 256), bf16), jnp.ones((16, 256), bf16)
    first_four = lax.broadcasted_iota(jnp.int32, (8, 128), 0) < 4

    def wide(row):
        return jnp.broadcast_to(row, (16, 256))

    def target_rows(i):
        rows = pl.ds(pl.multiple_of(i * 8, 8), 8)
        half, slot = i % 2, i // 2
        slot_core, outer, inner = slot // 16, (slot // 4) % 4, slot % 4
        slot_y = outer * (1 - slot_core) + inner * slot_core
        slot_z = inner * (1 - slot_core) + outer * slot_core
        offset = comb[slot_core, slot_z, slot_y, pl.ds(half, 1), :] - first
        inside = (offset >= 0) & (offset < COLS)
        tile = jnp.floor(offset * jnp.float32(1 / 128))
        column = offset - tile * 128
        tile = jnp.where(inside, tile, jnp.float32(-8))
        rest = comb[slot_core, slot_z, slot_y, pl.ds(2 + half, 1), :]
        parts = []
        for _ in range(3):
            parts.append(rest.astype(bf16).astype(jnp.float32))
            rest = rest - parts[-1]
        placed = []
        for k in range(2):
            at = slice(k * 256, (k + 1) * 256)
            tiles = jnp.where(same_token, wide(tile[:, at]), jnp.float32(-8)).astype(bf16) - tile_of_row[k]
            masks = [tiles == bf16(4 * j) for j in range(5)]
            left_side = [jnp.where(m, part, zero) for part in [wide(p[:, at]).astype(bf16) for p in parts] for m in masks]
            columns = wide(column[:, at]).astype(bf16) - column_of_row
            right_side = [jnp.where(columns == bf16(16 * j), one, zero) for j in range(8)]
            out = lax.dot_general(
                jnp.concatenate(left_side, axis=0), jnp.concatenate(right_side, axis=0), NT, preferred_element_type=jnp.float32)
            placed.append(out[0:80] + out[80:160] + out[160:240])
        for t in range(TILES):
            at, pair = slice(t * 128, (t + 1) * 128), slice(t // 2 * 8, t // 2 * 8 + 8)
            if t % 2 == 0:
                value = jnp.where(first_four, placed[0][pair], placed[1][pair])
            else:
                value = pltpu.roll(jnp.where(first_four, placed[1][pair], placed[0][pair]), 4, 0)
            target[rows, at] = value

    lane = lax.broadcasted_iota(jnp.int32, (16, 128), 1)

    def running(n, last=False):
        for r in range(0, TOK, 16):
            rows = slice(r, r + 16)
            values = [logits[rows, pl.ds(n * 256 if isinstance(n, int) else pl.multiple_of(n * 256, 256), 128)]]
            if last:
                values = [jnp.where(lane < TAIL, values[0], jnp.float32(-1e30))]
            else:
                at = n * 256 + 128
                values.append(logits[rows, pl.ds(at if isinstance(n, int) else pl.multiple_of(at, 128), 128)])
            peak = functools.reduce(jnp.maximum, values)
            old = top[rows, :]
            peak = jnp.maximum(old, peak)
            sums = functools.reduce(jnp.add, [jnp.exp(v - peak) for v in values])
            sums = sums + total[rows, :] * jnp.exp(old - peak)
            top[rows, :] = peak
            total[rows, :] = sums

    def logits_block(n, size):
        block = pl.ds(n * 256 if isinstance(n, int) else pl.multiple_of(n * 256, 256), size)
        logits[:, block] = lax.dot_general(h[...], w[block, :], NT, preferred_element_type=jnp.float32)

    def pairs(low, high, whole=True):
        @pl.loop(low, high)
        def _(k):
            w_copy(2 * k - 1).wait()
            w_copy(2 * k).wait()
            if whole:
                running(2 * k - 3)
            running(2 * k - 2)
            logits_block(2 * k - 1, 512)

    pltpu.make_async_copy(h, h, h_sem).wait()
    w_copy(0).wait()
    logits_block(0, 256)
    top[...] = jnp.full((TOK, 128), -1e30, jnp.float32)
    total[...] = jnp.zeros((TOK, 128), jnp.float32)
    pl.semaphore_wait(barrier, 16)
    start(comb_copies(0))
    pairs(1, 2, whole=False)
    pairs(2, 3)
    arrived(comb_copies(0))
    start(comb_copies(1))
    pairs(3, (NB + 1) // 2)
    w_tail().wait()
    w[COLS:, :] = jnp.zeros((PADDED - COLS, D), jnp.bfloat16)
    running(NB - 2)
    running(NB - 1)
    logits[:, MAIN:] = lax.dot_general(h[...], w[MAIN:, :], NT, preferred_element_type=jnp.float32)
    running(NB, last=True)

    def original_rows(col, i):
        return jnp.concatenate([col[pl.ds(slot_of(8 * i + j) * OWN, OWN), :] for j in range(8)], axis=0)

    def lse_rows(i):
        peaks, sums = jnp.transpose(original_rows(top, i)), jnp.transpose(original_rows(total, i))
        peak = jnp.max(peaks, axis=0, keepdims=True)
        return peak + jnp.log(jnp.sum(sums * jnp.exp(peaks - peak), axis=0, keepdims=True))

    stat_core[0, core] = jnp.concatenate([lse_rows(i) for i in range(4)], axis=0)
    start(stat_copies(0, 0))

    arrived(comb_copies(1))
    pl.loop(0, 16, unroll=8)(target_rows)
    arrived(stat_copies(0, 0))
    stat_chip[0, z * 4 + y] = log_add(stat_core[0])
    start(stat_copies(0, 1))
    pl.loop(16, TOK // 8, unroll=8)(target_rows)
    arrived(stat_copies(0, 1))
    log_total = log_add(stat_chip[0])
    for i in range(4):
        col = jnp.transpose(jnp.broadcast_to(log_total[i:i + 1, :], (128, 128)))
        for j in range(8):
            ltcol[pl.ds(slot_of(8 * i + j) * OWN, OWN), :] = col[j * OWN:(j + 1) * OWN, :]

    @pl.loop(0, TOK // 16, unroll=2)
    def _(i):
        rows = pl.ds(pl.multiple_of(i * 16, 16), 16)
        lt = ltcol[rows, :]
        terms = jnp.zeros((16, 128), jnp.float32)
        for t in range(TILES):
            at = slice(t * 128, (t + 1) * 128)
            logit, want = logits[rows, at], target[rows, at]
            terms = terms + want * logit
            value = jnp.exp(logit - lt) - want
            if t == TILES - 1:
                value = jnp.where(lane < TAIL, value, jnp.float32(0.0))
            gm[rows, at] = value.astype(jnp.bfloat16)
        cross[rows, :] = terms

    own_rows = pl.ds(pl.multiple_of(my_slot * OWN, OWN), OWN)
    cross[own_rows, :] = cross[own_rows, :] - jnp.where(lane == 0, negent, jnp.float32(0.0))

    def multiply(unit):
        c = max(k for k in range(NC) if sum(CHUNKS[:k]) <= unit)
        at = (unit - sum(CHUNKS[:c])) * UNIT
        part = jnp.dot(gm[...], w[:, unit * UNIT:(unit + 1) * UNIT], preferred_element_type=jnp.float32)
        g[c][:, :, :, :, at:at + UNIT] = part.reshape(2, 4, 4, OWN, UNIT)

    def step_core(c):
        return [remote(g[c].at[1 - core], cr[c], g_send.at[c, 0], g_recv.at[c, 0], mate)]

    def step_far(c):
        far = (a + 2) % 4
        return [
            remote(g[c].at[core, far, 0:2], r11[c].at[0], g_send.at[c, 1], g_recv.at[c, 1], device(a_right, b)),
            remote(g[c].at[core, far, 2:4], r11[c].at[1], g_send.at[c, 2], g_recv.at[c, 2], device(a_left, b)),
        ]

    def step_near(c):
        return [
            remote(g[c].at[core, a_right], r12[c].at[0], g_send.at[c, 3], g_recv.at[c, 3], device(a_right, b)),
            remote(g[c].at[core, a_left], r12[c].at[1], g_send.at[c, 4], g_recv.at[c, 4], device(a_left, b)),
        ]

    def step_far2(c):
        if c in STRAIGHT:
            return [
                remote(g[c].at[core, a, (b + d) % 4], r2[c].at[d - 1], g_send.at[c, 4 + d], g_recv.at[c, 4 + d], device(a, (b + d) % 4))
                for d in (1, 2, 3)
            ]
        far = (b + 2) % 4
        return [
            remote(g[c].at[core, a, far, 0:8], r2[c].at[2, 0:8], g_send.at[c, 5], g_recv.at[c, 5], device(a, b_right)),
            remote(g[c].at[core, a, far, 8:16], r2[c].at[2, 8:16], g_send.at[c, 6], g_recv.at[c, 6], device(a, b_left)),
        ]

    def step_near2(c):
        return [
            remote(g[c].at[core, a, b_right], r2[c].at[0], g_send.at[c, 7], g_recv.at[c, 7], device(a, b_right)),
            remote(g[c].at[core, a, b_left], r2[c].at[1], g_send.at[c, 8], g_recv.at[c, 8], device(a, b_left)),
        ]

    unit = 0
    for event in ORDER:
        if event == "m":
            multiply(unit)
            unit += 1
            continue
        kind, c = event[0], int(event[1])
        if kind == "C":
            start(step_core(c))
        elif kind == "X":
            arrived(step_core(c))
            for k in range(4):
                g[c][core, k] = g[c][core, k] + cr[c][k]
            start(step_far(c))
        elif kind == "Y":
            arrived(step_far(c))
            g[c][core, a_right, 0:2] = g[c][core, a_right, 0:2] + r11[c][0]
            g[c][core, a_left, 2:4] = g[c][core, a_left, 2:4] + r11[c][1]
            start(step_near(c))
        elif kind == "Z":
            arrived(step_near(c))
            g[c][core, a] = g[c][core, a] + (r12[c][0] + r12[c][1])
            start(step_far2(c))
        elif kind == "W":
            arrived(step_far2(c))
            g[c][core, a, b_right, 0:8] = g[c][core, a, b_right, 0:8] + r2[c][2, 0:8]
            g[c][core, a, b_left, 8:16] = g[c][core, a, b_left, 8:16] + r2[c][2, 8:16]
            start(step_near2(c))
        elif kind == "F":
            arrived(step_far2(c) if c in STRAIGHT else step_near2(c))
            at = sum(CHUNKS[:c]) * UNIT
            value = g[c][core, a, b] + (r2[c][0] + r2[c][1])
            if c in STRAIGHT:
                value = value + r2[c][2]
            grad_out[:, at:at + CHUNKS[c] * UNIT] = value
        elif c == 1:
            rows = [jnp.sum(jnp.transpose(original_rows(cross, i)), axis=0, keepdims=True) for i in range(4)]
            stat_core[1, core] = jnp.concatenate(rows, axis=0)
            start(stat_copies(1, 0))
        elif c == 2:
            arrived(stat_copies(1, 0))
            stat_chip[1, z * 4 + y] = jnp.sum(stat_core[1], axis=0)
            start(stat_copies(1, 1))
        else:
            arrived(stat_copies(1, 1))
            loss_out[...] = log_total - jnp.sum(stat_chip[1], axis=0)

    for k in range(2):
        left(comb_copies(k) + stat_copies(0, k) + stat_copies(1, k))
    for c in range(NC):
        left(step_core(c) + step_far(c) + step_near(c) + step_far2(c) + ([] if c in STRAIGHT else step_near2(c)))


def finish(grad_ref, loss_ref, grad_out, loss_out):
    grad_out[...] = grad_ref[...]
    loss_out[...] = loss_ref[...]


def local(hidden, head_weight, teacher_ids, teacher_logits):
    any_space = pl.BlockSpec(memory_space=pl.ANY)
    vmem = pl.BlockSpec(memory_space=pltpu.VMEM)
    f32, bf16 = jnp.float32, jnp.bfloat16
    dma = pltpu.SemaphoreType.DMA
    widths = [k * UNIT for k in CHUNKS]
    grad, loss = pl.pallas_call(
        kernel,
        out_shape=(jax.ShapeDtypeStruct((OWN, D), f32), jax.ShapeDtypeStruct((4, 128), f32)),
        in_specs=[any_space, any_space, vmem, vmem],
        out_specs=(vmem, vmem),
        scratch_shapes=[
            pltpu.VMEM((PADDED, D), bf16),
            pltpu.VMEM((TOK, D), bf16),
            pltpu.VMEM((TOK, PADDED), f32),
            pltpu.VMEM((TOK, PADDED), f32),
            pltpu.VMEM((TOK, PADDED), bf16),
            [pltpu.VMEM((2, 4, 4, OWN, k), f32) for k in widths],
            [pltpu.VMEM((4, 4, OWN, k), f32) for k in widths],
            [pltpu.VMEM((2, 2, OWN, k), f32) for k in widths],
            [pltpu.VMEM((2, 4, OWN, k), f32) for k in widths],
            [pltpu.VMEM((3, OWN, k), f32) for k in widths],
            pltpu.VMEM((2, 4, 4, 4, 8 * K), f32),
            pltpu.VMEM((2, 2, 4, 128), f32),
            pltpu.VMEM((2, 16, 4, 128), f32),
            pltpu.VMEM((TOK, 128), f32),
            pltpu.VMEM((TOK, 128), f32),
            pltpu.VMEM((TOK, 128), f32),
            pltpu.VMEM((TOK, 128), f32),
            dma, dma((NB + 1,)), dma((16,)), dma((16,)), dma((2, 16)), dma((2, 16)), dma((NC, 9)), dma((NC, 9)),
        ],
        compiler_params=pltpu.CompilerParams(
            collective_id=0, has_side_effects=True, vmem_limit_bytes=60 * 1024 * 1024),
    )(hidden, head_weight.T, teacher_ids, teacher_logits)
    grad, loss = pl.pallas_call(
        finish,
        out_shape=(jax.ShapeDtypeStruct((OWN, D), f32), jax.ShapeDtypeStruct((4, 128), f32)),
        in_specs=[vmem, vmem],
        out_specs=(vmem, vmem),
    )(grad, loss)
    return loss.reshape(TOK), grad


def solution(mesh):
    placed = (P("dp", None), P(None, "vocab"), P(("dp", "vocab"), None), P(("dp", "vocab"), None))
    return jax.shard_map(
        local,
        mesh=mesh,
        in_specs=placed,
        out_specs=(P("dp"), P(("dp", "vocab"), None)),
        check_vma=False,
    )
```

time: 75.3 us -> 70.8 us (0.940)
  local copies, waits for them, and re-layouts: 2.89 us -> 0 us
  Pallas kernels: 71.4 us -> 69.9 us
    pallas_call x1, Pallas kernels: 71.4 us -> 68.3 us  [local(): pl.pallas_call(kernel, out_shape=(jax.ShapeDtypeStruct((OWN, D), f32), ja...]
    unnamed x2 -> x0, local copies, waits for them, and re-layouts: 2.89 us -> none
    pallas_call x0 -> x1, Pallas kernels: none -> 1.65 us  [local(): pl.pallas_call(finish, out_shape=(jax.ShapeDtypeStruct((OWN, D), f32), ja...]
where the time goes in v3:
time: 70.8 us; the launch traced here: 70.6 us
  Pallas kernels  69.9 us (99%)
    pallas_call x1, Pallas kernels, local(): pl.pallas_call(kernel, out_shape=(jax.ShapeDtypeStruct((OWN, D), f32), ja...  68.3 us
    pallas_call x1, Pallas kernels, local(): pl.pallas_call(finish, out_shape=(jax.ShapeDtypeStruct((OWN, D), f32), ja...  1.65 us

profile of v3, /device:TPU:0, one launch (start us, length us, event | category | flops | bytes accessed | tf_op | source)
XLA Modules:
  0.0 70.6 jit_solution(11055497866422972512)
XLA Ops:
  0.6 68.3 %shard_map.59 = (f32[16,3584]{1,0:T(8,128)}, f32[4,128]{1,0:T(4,128)}) custom-call(bf16[512,3584]{1,0:T(8,128)(2,1)} %hidden.1, bf16[2376,3584]{1,0:T(8,128)(2,1)} %bitcast.2, s32[16,64]{1,0:T(8,128)} %ids_ref.1, f32[16,64]{1,0:T(8,128)} %tlog_ref.1), custom_call_target="tpu_custom_call" | custom-call | tf_op jit(solution)/shard_map/pallas_call | solution.py:386
  68.9 1.6 %shard_map.60 = (f32[16,3584]{1,0:T(8,128)}, f32[4,128]{1,0:T(4,128)}) custom-call(f32[16,3584]{1,0:T(8,128)} %get-tuple-element.6.grad_ref, f32[4,128]{1,0:T(4,128)} %get-tuple-element.7.loss_ref), custom_call_target="tpu_custom_call" | custom-call | tf_op jit(solution)/shard_map/pallas_call | solution.py:414

commit v4 on v3

--- a/solution.py
+++ b/solution.py
@@ -19,15 +19,14 @@
 TILES = PADDED // 128
 NB = MAIN // 256
 UNIT = 256
-CHUNKS = (1, 2, 3, 3, 3, 2)
+CHUNKS = (3, 4, 4, 3)
 NC = len(CHUNKS)
-STRAIGHT = (4, 5)
+STRAIGHT = (2, 3)
 K = 64
 ORDER = (
-    "m", "m", "m", "C1", "C0", "m", "m", "X1", "m", "C2", "X0", "m", "m", "X2", "m", "C3", "Y1",
-    "m", "Y0", "m", "X3", "m", "C4", "Y2", "m", "m", "X4", "C5", "Y3", "K1", "Z2", "X5", "Z0", "Y4",
-    "Z3", "Y5", "Z1", "W0", "W2", "Z4", "W3", "Z5", "W1", "K2", "F4", "F3", "F2", "F0", "F5", "K3",
-    "F1",
+    "m", "m", "m", "C0", "m", "m", "X0", "m", "m", "C1", "m", "m", "X1", "Y0", "m", "m", "C2", "m",
+    "m", "X2", "Y1", "m", "C3", "X3", "Y2", "K1", "Z0", "Y3", "Z1", "K2", "Z2", "W0", "Z3", "W1",
+    "K3", "F0", "F1", "F2", "F3",
 )
 NT = (((1,), (1,)), ((), ()))
 
@@ -38,11 +37,11 @@
 
 
 def kernel(
-    hidden, weight, ids_ref, tlog_ref,
+    hidden, weight, ids_hbm, tlog_hbm,
     grad_out, loss_out,
     w, h, logits, target, gm, g, cr, r11, r12, r2,
     comb, stat_core, stat_chip, ltcol, top, total, cross,
-    h_sem, w_sem, comb_send, comb_recv, st_send, st_recv, g_send, g_recv,
+    ids_ref, tlog_ref, t_sem, h_sem, w_sem, comb_send, comb_recv, st_send, st_recv, g_send, g_recv,
 ):
     me = lax.axis_index("vocab")
     core = me % 2
@@ -81,10 +80,6 @@
         for copy in copies:
             copy.wait_send()
 
-    for v in range(NV):
-        s = slot_of(v)
-        pltpu.make_async_copy(hidden.at[pl.ds(v * OWN, OWN)], h.at[pl.ds(s * OWN, OWN)], h_sem).start()
-
     def w_copy(n):
         rows = pl.ds(n * 256, 256)
         return pltpu.make_async_copy(weight.at[rows], w.at[rows], w_sem.at[n])
@@ -93,13 +88,24 @@
         rows = pl.ds(MAIN, TAIL)
         return pltpu.make_async_copy(weight.at[rows], w.at[rows], w_sem.at[NB])
 
-    for n in range(NB):
+    teacher = [
+        pltpu.make_async_copy(ids_hbm, ids_ref, t_sem.at[0]),
+        pltpu.make_async_copy(tlog_hbm, tlog_ref, t_sem.at[1]),
+    ]
+    start(teacher)
+    w_copy(0).start()
+    for k in range(4):
+        pltpu.make_async_copy(hidden.at[:, k, 0], h.at[0, k], h_sem).start()
+        pltpu.make_async_copy(hidden.at[k, :, 1], h.at[1, k], h_sem).start()
+    for n in range(1, NB):
         w_copy(n).start()
     w_tail().start()
 
     barrier = pltpu.get_barrier_semaphore()
     for where in [mate] + [chip(dy, dz) for dy, dz in others]:
         pl.semaphore_signal(barrier, inc=1, device_id=where, device_id_type=MESH)
+    for copy in teacher:
+        copy.wait()
     tl = tlog_ref[...]
     shifted = tl - jnp.max(tl, axis=1, keepdims=True)
     log_probs = shifted - jnp.log(jnp.sum(jnp.exp(shifted), axis=1, keepdims=True))
@@ -206,7 +212,7 @@
 
     def logits_block(n, size):
         block = pl.ds(n * 256 if isinstance(n, int) else pl.multiple_of(n * 256, 256), size)
-        logits[:, block] = lax.dot_general(h[...], w[block, :], NT, preferred_element_type=jnp.float32)
+        logits[:, block] = lax.dot_general(h[...].reshape(TOK, D), w[block, :], NT, preferred_element_type=jnp.float32)
 
     def pairs(low, high, whole=True):
         @pl.loop(low, high)
@@ -223,18 +229,18 @@
     logits_block(0, 256)
     top[...] = jnp.full((TOK, 128), -1e30, jnp.float32)
     total[...] = jnp.zeros((TOK, 128), jnp.float32)
+    pairs(1, 2, whole=False)
+    pairs(2, 3)
     pl.semaphore_wait(barrier, 16)
     start(comb_copies(0))
-    pairs(1, 2, whole=False)
-    pairs(2, 3)
+    pairs(3, (NB + 1) // 2)
     arrived(comb_copies(0))
     start(comb_copies(1))
-    pairs(3, (NB + 1) // 2)
     w_tail().wait()
     w[COLS:, :] = jnp.zeros((PADDED - COLS, D), jnp.bfloat16)
     running(NB - 2)
     running(NB - 1)
-    logits[:, MAIN:] = lax.dot_general(h[...], w[MAIN:, :], NT, preferred_element_type=jnp.float32)
+    logits[:, MAIN:] = lax.dot_general(h[...].reshape(TOK, D), w[MAIN:, :], NT, preferred_element_type=jnp.float32)
     running(NB, last=True)
 
     def original_rows(col, i):
@@ -386,11 +392,11 @@
     grad, loss = pl.pallas_call(
         kernel,
         out_shape=(jax.ShapeDtypeStruct((OWN, D), f32), jax.ShapeDtypeStruct((4, 128), f32)),
-        in_specs=[any_space, any_space, vmem, vmem],
+        in_specs=[any_space] * 4,
         out_specs=(vmem, vmem),
         scratch_shapes=[
             pltpu.VMEM((PADDED, D), bf16),
-            pltpu.VMEM((TOK, D), bf16),
+            pltpu.VMEM((2, 4, 4, OWN, D), bf16),
             pltpu.VMEM((TOK, PADDED), f32),
             pltpu.VMEM((TOK, PADDED), f32),
             pltpu.VMEM((TOK, PADDED), bf16),
@@ -406,11 +412,13 @@
             pltpu.VMEM((TOK, 128), f32),
             pltpu.VMEM((TOK, 128), f32),
             pltpu.VMEM((TOK, 128), f32),
-            dma, dma((NB + 1,)), dma((16,)), dma((16,)), dma((2, 16)), dma((2, 16)), dma((NC, 9)), dma((NC, 9)),
+            pltpu.VMEM((OWN, K), jnp.int32),
+            pltpu.VMEM((OWN, K), f32),
+            dma((2,)), dma, dma((NB + 1,)), dma((16,)), dma((16,)), dma((2, 16)), dma((2, 16)), dma((NC, 9)), dma((NC, 9)),
         ],
         compiler_params=pltpu.CompilerParams(
             collective_id=0, has_side_effects=True, vmem_limit_bytes=60 * 1024 * 1024),
-    )(hidden, head_weight.T, teacher_ids, teacher_logits)
+    )(hidden.reshape(4, 4, 2, OWN, D), head_weight.T, teacher_ids, teacher_logits)
     grad, loss = pl.pallas_call(
         finish,
         out_shape=(jax.ShapeDtypeStruct((OWN, D), f32), jax.ShapeDtypeStruct((4, 128), f32)),

time: 70.8 us -> 67.4 us (0.952)
  Pallas kernels: 69.9 us -> 66.2 us
    pallas_call x1, Pallas kernels: 68.3 us -> 64.5 us  [local(): pl.pallas_call(kernel, out_shape=(jax.ShapeDtypeStruct((OWN, D), f32), ja...]
where the time goes in v4:
time: 67.4 us; the launch traced here: 66.8 us
  Pallas kernels  66.2 us (98%)
    pallas_call x1, Pallas kernels, local(): pl.pallas_call(kernel, out_shape=(jax.ShapeDtypeStruct((OWN, D), f32), ja...  64.5 us
    pallas_call x1, Pallas kernels, local(): pl.pallas_call(finish, out_shape=(jax.ShapeDtypeStruct((OWN, D), f32), ja...  1.65 us

profile of v4, /device:TPU:0, one launch (start us, length us, event | category | flops | bytes accessed | tf_op | source)
XLA Modules:
  0.0 66.8 jit_solution(12513821506475586811)
XLA Ops:
  0.6 64.5 %shard_map.59 = (f32[16,3584]{1,0:T(8,128)}, f32[4,128]{1,0:T(4,128)}) custom-call(bf16[4,4,2,16,3584]{4,3,2,1,0:T(8,128)(2,1)} %bitcast.4, bf16[2376,3584]{1,0:T(8,128)(2,1)} %bitcast.3, s32[16,64]{1,0:T(8,128)} %ids_hbm.1, f32[16,64]{1,0:T(8,128)} %tlog_hbm.1), custom_call_target="tpu_custom_call" | custom-call | tf_op jit(solution)/shard_map/pallas_call | solution.py:392
  65.2 1.6 %shard_map.60 = (f32[16,3584]{1,0:T(8,128)}, f32[4,128]{1,0:T(4,128)}) custom-call(f32[16,3584]{1,0:T(8,128)} %get-tuple-element.6.grad_ref, f32[4,128]{1,0:T(4,128)} %get-tuple-element.7.loss_ref), custom_call_target="tpu_custom_call" | custom-call | tf_op jit(solution)/shard_map/pallas_call | solution.py:422

commit v5 on v4

--- a/solution.py
+++ b/solution.py
@@ -24,9 +24,7 @@
 STRAIGHT = (2, 3)
 K = 64
 ORDER = (
-    "m", "m", "m", "C0", "m", "m", "X0", "m", "m", "C1", "m", "m", "X1", "Y0", "m", "m", "C2", "m",
-    "m", "X2", "Y1", "m", "C3", "X3", "Y2", "K1", "Z0", "Y3", "Z1", "K2", "Z2", "W0", "Z3", "W1",
-    "K3", "F0", "F1", "F2", "F3",
+    "m", "m", "m", "C0", "m", "m", "X0", "m", "m", "C1", "m", "m", "X1", "Y0", "m", "m", "C2", "m", "m", "X2", "Y1", "m", "C3", "X3", "Y2", "K1", "Z0", "Y3", "Z1", "Z2", "W0", "K2", "Z3", "W1", "F0", "F1", "K3", "F2", "F3",
 )
 NT = (((1,), (1,)), ((), ()))
 
@@ -255,11 +253,11 @@
     start(stat_copies(0, 0))
 
     arrived(comb_copies(1))
-    pl.loop(0, 16, unroll=8)(target_rows)
+    pl.loop(0, 8, unroll=8)(target_rows)
     arrived(stat_copies(0, 0))
     stat_chip[0, z * 4 + y] = log_add(stat_core[0])
     start(stat_copies(0, 1))
-    pl.loop(16, TOK // 8, unroll=8)(target_rows)
+    pl.loop(8, TOK // 8, unroll=8)(target_rows)
     arrived(stat_copies(0, 1))
     log_total = log_add(stat_chip[0])
     for i in range(4):

time: 67.4 us -> 68.2 us (1.012)
  Pallas kernels: 66.2 us -> 67.5 us
    pallas_call x1, Pallas kernels: 64.5 us -> 65.8 us  [local(): pl.pallas_call(kernel, out_shape=(jax.ShapeDtypeStruct((OWN, D), f32), ja...]
where the time goes in v5:
time: 68.2 us; the launch traced here: 68.1 us
  Pallas kernels  67.5 us (99%)
    pallas_call x1, Pallas kernels, local(): pl.pallas_call(kernel, out_shape=(jax.ShapeDtypeStruct((OWN, D), f32), ja...  65.8 us
    pallas_call x1, Pallas kernels, local(): pl.pallas_call(finish, out_shape=(jax.ShapeDtypeStruct((OWN, D), f32), ja...  1.65 us

profile of v5, /device:TPU:0, one launch (start us, length us, event | category | flops | bytes accessed | tf_op | source)
XLA Modules:
  0.0 68.1 jit_solution(13308147385778208844)
XLA Ops:
  0.6 65.8 %shard_map.59 = (f32[16,3584]{1,0:T(8,128)}, f32[4,128]{1,0:T(4,128)}) custom-call(bf16[4,4,2,16,3584]{4,3,2,1,0:T(8,128)(2,1)} %bitcast.4, bf16[2376,3584]{1,0:T(8,128)(2,1)} %bitcast.3, s32[16,64]{1,0:T(8,128)} %ids_hbm.1, f32[16,64]{1,0:T(8,128)} %tlog_hbm.1), custom_call_target="tpu_custom_call" | custom-call | tf_op jit(solution)/shard_map/pallas_call | solution.py:390
  66.5 1.6 %shard_map.60 = (f32[16,3584]{1,0:T(8,128)}, f32[4,128]{1,0:T(4,128)}) custom-call(f32[16,3584]{1,0:T(8,128)} %get-tuple-element.6.grad_ref, f32[4,128]{1,0:T(4,128)} %get-tuple-element.7.loss_ref), custom_call_target="tpu_custom_call" | custom-call | tf_op jit(solution)/shard_map/pallas_call | solution.py:420
